TPU v7x, 32 devices: a whole 2x2x4 slice. The times are simulated.
32 devices in a mesh: tm: 4 (over z), space: 8 (over y, x, core).
Axes of the slice: x: 2, y: 2, z: 4, core: 2. Of those that a mesh axis runs over, the one named last changes fastest.
Arguments:
- hindcast_archive: bfloat16 [4, 4, 16, 4, 8192], P('tm', None, None, None, 'space'), may hold values from -6 to 6
- op_blocks: bfloat16 [4, 768, 128, 128], P('tm', 'space'), may hold values from -0.5 to 0.5
- block_index: int32 [4, 768], P('tm', 'space'), may hold values from 0 to 11
- obs_values: bfloat16 [4, 4, 98304], P('tm', None, 'space'), may hold values from -6 to 6
- obs_weights: bfloat16 [4, 4, 98304], P('tm', None, 'space'), may hold values from 0.049804688 to 0.5
- obs_counts: int32 [4, 8], P('tm', 'space'), may hold values from 3072 to 12288, as said below
Outputs:
- gradient: float32 [4, 16, 4, 8192], P('tm', None, None, 'space')
Inputs may be any that keep to these rules, and one draw needn't show every extreme that they name: `block_index`: A value below 2 names one of the last 2 blocks of the tile before, a value from 2 to 9 one of the tile's own blocks, a larger one the first blocks of the tile after. `obs_counts`: in every valid time some tile has all 12288 slots live; the live observations of a tile are its first slots.
All inputs are finite; a program needn't handle non-finite values.
Results may differ from a plain program's by a relative error of at most 0.0014.
Values may be sent and summed in bfloat16 or wider, within the bound.
A program may use at most 128 MiB of HBM per device.

v0:
```python
import jax
import jax.numpy as jnp
from jax import lax
from jax.sharding import PartitionSpec as P

GROUP_SITE_SPAN = 128
EDGE = 2


def with_halo(block, sides, width):
    for axis, dim in sides:
        count = lax.axis_size(axis)
        forward = [(i, i + 1) for i in range(count - 1)]
        forward.append((count - 1, 0))
        backward = [(target, source) for source, target in forward]
        low = lax.ppermute(
            lax.slice_in_dim(block, block.shape[dim] - width, None, axis=dim), axis, forward
        )
        high = lax.ppermute(lax.slice_in_dim(block, 0, width, axis=dim), axis, backward)
        block = jnp.concatenate([low, block, high], axis=dim)
    return block


def passed_along(value, axis, steps):
    count = lax.axis_size(axis)
    pairs = [(source, (source + steps) % count) for source in range(count)]
    return lax.ppermute(value, axis, pairs)


def extend(grouped):
    return with_halo(grouped, (("space", 4),), EDGE * GROUP_SITE_SPAN)


def observe(extended, operator, indices, values, weights, counts):
    block_width = operator.shape[-1]
    lead_shape = extended.shape[:-1]
    blocks = extended.reshape(-1, extended.shape[-1] // block_width, block_width)
    collected_entries = jnp.take(blocks, indices, axis=1)
    images = jnp.einsum(
        "bij,cbj->cbi", operator, collected_entries, preferred_element_type=jnp.float32
    )
    obs_blocks = indices.shape[0]
    field_count = values.shape[0]
    images = images.reshape(-1, field_count, obs_blocks, block_width)
    position = lax.broadcasted_iota(
        jnp.int32, (obs_blocks, block_width), 0
    ) * block_width + lax.broadcasted_iota(jnp.int32, (obs_blocks, block_width), 1)
    live_mask = (position < counts[0]).astype(jnp.float32)
    observed = values.reshape(field_count, obs_blocks, block_width).astype(jnp.float32)
    scaling = weights.reshape(field_count, obs_blocks, block_width).astype(jnp.float32)
    misfit = ((images - observed) * scaling * live_mask).astype(jnp.bfloat16)
    misfit = misfit.reshape(-1, obs_blocks, block_width)
    adjoint = jnp.einsum("bij,cbi->cbj", operator, misfit, preferred_element_type=jnp.float32)
    selector = (indices[:, None] == jnp.arange(blocks.shape[1], dtype=jnp.int32)[None, :]).astype(
        jnp.float32
    )
    cell_sums = jnp.einsum("cbj,bk->ckj", adjoint, selector, precision=lax.Precision.HIGHEST)
    return cell_sums.reshape(lead_shape + (extended.shape[-1],))


def settle(adjoint_ext):
    rim_width = EDGE * GROUP_SITE_SPAN
    lower_rim = adjoint_ext[..., :rim_width]
    upper_rim = adjoint_ext[..., -rim_width:]
    interior = adjoint_ext[..., rim_width:-rim_width]
    from_above = passed_along(lower_rim, "space", -1)
    from_below = passed_along(upper_rim, "space", 1)
    interior = interior.at[..., -rim_width:].add(from_above)
    return interior.at[..., :rim_width].add(from_below)


def body(hindcast_archive, op_blocks, block_index, obs_values, obs_weights, obs_counts):
    tm_size = lax.axis_size("tm")
    lead_count = hindcast_archive.shape[1]
    regrouped = [hindcast_archive[:, 0]]
    for horizon_step in range(1, lead_count):
        regrouped.append(
            passed_along(
                hindcast_archive[:, horizon_step], "tm", horizon_step * tm_size // lead_count
            )
        )
    extended = extend(jnp.stack(regrouped, axis=1))
    adjoint_ext = jnp.stack(
        [
            observe(
                extended[0],
                op_blocks[0],
                block_index[0],
                obs_values[0],
                obs_weights[0],
                obs_counts[0],
            )
        ]
    )
    interior = settle(adjoint_ext)
    running = interior[:, 0]
    for horizon_step in range(1, lead_count):
        running = running + passed_along(
            interior[:, horizon_step], "tm", -(horizon_step * tm_size // lead_count)
        )
    return running


def solution(mesh):
    in_specs = (
        P("tm", None, None, None, "space"),
        P("tm", "space", None, None),
        P("tm", "space"),
        P("tm", None, "space"),
        P("tm", None, "space"),
        P("tm", "space"),
    )
    out_specs = P("tm", None, None, "space")
    return jax.shard_map(body, mesh=mesh, in_specs=in_specs, out_specs=out_specs, check_vma=False)
```

profile of v0, /device:TPU:0, one launch (start us, length us, event | category | flops | bytes accessed | tf_op | source)
XLA Modules:
  0.0 120.3 jit_solution(16703642495392455104)
XLA Ops:
  0.0 1.4 %fusion.41 = (bf16[1,1,16,4,1024]{4,3,2,1,0:T(4,128)(2,1)S(1)}, bf16[1,16,4,1024]{3,2,1,0:T(4,128)(2,1)S(1)}, bf16[1,16,4,1024]{3,2,1,0:T(4,128)(2,1)S(1)}, bf16[1,16,4,1024]{3,2,1,0:T(4,128)(2,1)S(1)}) fusion(bf16[1,4,16,4,1024]{4,3,2,1,0:T(4,128)(2,1)} %param.10), kind=kLoop, calls=%fused_computation.52 | loop fusion | bytes 1048576 | tf_op jit(solution)/shard_map/slice | solution.py:75
  1.4 3.1 %collective-permute-start = (bf16[1,16,4,1024]{3,2,1,0:T(4,128)(2,1)S(1)}, bf16[1,16,4,1024]{3,2,1,0:T(4,128)(2,1)S(1)}, u32[]{:S(2)}, u32[]{:S(2)}) collective-permute-start(bf16[1,16,4,1024]{3,2,1,0:T(4,128)(2,1)S(1)} %get-tuple-element.37), channel_id=1, source_target_pairs={{0,8},{8,16},{16,24},{24,0},{1,9},{9,17},{17,25},{25,1},{2,10},{10... | collective-permute-start | bytes 393224 | tf_op jit(solution)/shard_map/ppermute | solution.py:27
  4.5 2.1 %collective-permute-start.2 = (bf16[1,16,4,1024]{3,2,1,0:T(4,128)(2,1)S(1)}, bf16[1,16,4,1024]{3,2,1,0:T(4,128)(2,1)S(1)}, u32[]{:S(2)}, u32[]{:S(2)}) collective-permute-start(bf16[1,16,4,1024]{3,2,1,0:T(4,128)(2,1)S(1)} %get-tuple-element.38), channel_id=1, source_target_pairs={{0,24},{8,0},{16,8},{24,16},{1,25},{9,1},{17,9},{25,17},{2,26},{10... | collective-permute-start | bytes 393224 | tf_op jit(solution)/shard_map/ppermute | solution.py:27
  6.6 0.9 collective-permute-start.1
  8.2 0.9 bitcast_convert_fusion.1
  9.1 0.9 bitcast_convert_fusion
  10.1 0.7 fusion.33
  10.8 0.7 compare_and_fusion
  11.4 0.9 collective-permute-done.2
  12.3 6.2 %collective-permute-done.1 = bf16[1,16,4,1024]{3,2,1,0:T(4,128)(2,1)S(1)} collective-permute-done((bf16[1,16,4,1024]{3,2,1,0:T(4,128)(2,1)S(1)}, bf16[1,16,4,1024]{3,2,1,0:T(4,128)(2,1)S(1)}, u32[]{:S(2)}, u32[]{:S(2)}) %collective-permute-start.1) | collective-permute-done | bytes 131104 | tf_op jit(solution)/shard_map/ppermute | solution.py:27
  18.7 2.6 %collective-permute-start.4 = (bf16[1,4,16,4,256]{4,3,2,1,0:T(4,128)(2,1)S(1)}, bf16[1,4,16,4,256]{4,3,2,1,0:T(4,128)(2,1)S(1)}, u32[]{:S(2)}, u32[]{:S(2)}) collective-permute-start(bf16[1,4,16,4,256]{4,3,2,1,0:T(4,128)(2,1)S(1)} %get-tuple-element.35), channel_id=1, source_target_pairs={{1,0},{2,1},{3,2},{4,3},{5,4},{6,5},{7,6},{0,7},{9,8},{10,9},{11,1... | collective-permute-start | bytes 393224 | tf_op jit(solution)/shard_map/ppermute | solution.py:19
  21.3 0.7 fusion.37
  21.9 2.0 %collective-permute-done.3 = bf16[1,4,16,4,256]{4,3,2,1,0:T(4,128)(2,1)S(1)} collective-permute-done((bf16[1,4,16,4,256]{4,3,2,1,0:T(4,128)(2,1)S(1)}, bf16[1,4,16,4,256]{4,3,2,1,0:T(4,128)(2,1)S(1)}, u32[]{:S(2)}, u32[]{:S(2)}) %collective-permute-start.3) | collective-permute-done | bytes 131104 | tf_op jit(solution)/shard_map/ppermute | solution.py:16
  23.9 1.3 %pad_maximum_fusion = bf16[1,4,16,4,1536]{4,3,2,1,0:T(4,128)(2,1)} fusion(bf16[1,4,16,4,256]{4,3,2,1,0:T(4,128)(2,1)S(1)} %collective-permute-done.4, bf16[1,1,16,4,1024]{4,3,2,1,0:T(4,128)(2,1)S(1)} %bitcast.79, bf16[1,1,16,4,1024]{4,3,2,1,0:T(4,128)(2,1)S(1)} %bitcast.81, bf16[1,1,16,4,1024]{4,3,2,1,0:T(4,128)(2,1)S(1)} %bitcast.77, ...), kind=kLoop, calls=%fused_computation.18 | loop fusion | flops 4718592 | bytes 1572864 | tf_op jit(solution)/shard_map/concatenate | solution.py:20
  25.2 2.6 %reshape_squeeze.2 = bf16[256,12,128]{2,1,0:T(8,128)(2,1)} reshape(bf16[1,4,16,4,1536]{4,3,2,1,0:T(4,128)(2,1)} %pad_maximum_fusion) | data formatting | bytes 1572864 | tf_op jit(solution)/shard_map/reshape;squeeze | solution.py:37
  27.8 2.4 %copy.9 = bf16[256,12,128]{2,0,1:T(8,128)(2,1)} copy(bf16[256,12,128]{2,1,0:T(8,128)(2,1)} %reshape_squeeze.2) | data formatting | bytes 1572864 | tf_op jit(solution)/shard_map/reshape;squeeze | solution.py:37
  30.2 7.1 %gather_fusion = bf16[96,256,128]{2,1,0:T(8,128)(2,1)} fusion(bf16[256,12,128]{2,0,1:T(8,128)(2,1)} %copy.9, s32[1024]{0:T(1024)S(1)} %pad_clamp_fusion), kind=kCustom, calls=%fused_computation | custom fusion | bytes 12583296 | tf_op jit(solution)/shard_map/jit(_take)/gather | solution.py:38
  37.3 6.1 %mul.27 = f32[64,4,96,128]{3,1,0,2:T(4,128)} broadcast(f32[4,96,128]{2,0,1:T(4,128)S(1)} %bitcast_convert_fusion), dimensions={1,2,3} | broadcast | bytes 12779520 | tf_op jit(solution)/shard_map/mul | solution.py:51
  43.4 6.2 %sub.11 = f32[64,4,96,128]{3,1,0,2:T(4,128)} broadcast(f32[4,96,128]{2,0,1:T(4,128)S(1)} %bitcast_convert_fusion.1), dimensions={1,2,3} | broadcast | bytes 12779520 | tf_op jit(solution)/shard_map/sub | solution.py:51
  49.6 17.1 %fusion.6 = f32[96,256,128]{2,1,0:T(8,128)} fusion(f32[256,96,128]{2,0,1:T(8,128)} %bitcast.74, f32[256,96,128]{2,0,1:T(8,128)} %bitcast.75, f32[96,128]{1,0:T(8,128)S(1)} %copy-done.1, bf16[1,96,128,128]{3,2,1,0:T(8,128)(2,1)S(1)} %copy-done, bf16[96,256,128]{2,1,0:T(8,128)(2,1)} %gather_fusion, pred[96]{0:T(512)(128)(4,1)S(1)} %compare_and_fusion), kind=kOutput, calls=%fused_computation.8 | convolution fusion | flops 1626341376 | bytes 47235168 | tf_op jit(solution)/shard_map/bij,cbi->cbj/dot_general | solution.py:53
  66.7 16.2 %fusion.25 = f32[256,12,128]{2,1,0:T(8,128)} fusion(f32[96,256,128]{2,1,0:T(8,128)} %fusion.6, s32[96]{0:T(128)S(1)} %bitcast.82), kind=kOutput, calls=%fused_computation.17 | convolution fusion | flops 452985984 | bytes 14156160 | tf_op jit(solution)/shard_map/cbj,bk->ckj/dot_general | solution.py:57
  83.0 2.8 %stack_reshape.3 = f32[1,4,16,4,1536]{4,3,2,1,0:T(4,128)} reshape(f32[256,12,128]{2,1,0:T(8,128)} %fusion.25) | data formatting | bytes 3145728 | tf_op jit(solution)/shard_map/stack;reshape | solution.py:83
  85.7 1.1 fusion.40
  86.8 2.7 %collective-permute-start.5 = (f32[1,4,16,4,256]{4,3,2,1,0:T(4,128)S(1)}, f32[1,4,16,4,256]{4,3,2,1,0:T(4,128)S(1)}, u32[]{:S(2)}, u32[]{:S(2)}) collective-permute-start(f32[1,4,16,4,256]{4,3,2,1,0:T(4,128)S(1)} %get-tuple-element.30), channel_id=1, source_target_pairs={{0,7},{1,0},{2,1},{3,2},{4,3},{5,4},{6,5},{7,6},{8,15},{9,8},{10,9... | collective-permute-start | bytes 786440 | tf_op jit(solution)/shard_map/ppermute | solution.py:27
  89.5 1.3 %slice.125 = f32[1,4,16,4,1024]{4,3,2,1,0:T(4,128)S(1)} slice(f32[1,4,16,4,1536]{4,3,2,1,0:T(4,128)} %stack_reshape.3), slice={[0:1], [0:4], [0:16], [0:4], [256:1280]} | slice | bytes 2097152 | tf_op jit(solution)/shard_map/slice | solution.py:65
  90.8 5.1 %collective-permute-done.5 = f32[1,4,16,4,256]{4,3,2,1,0:T(4,128)S(1)} collective-permute-done((f32[1,4,16,4,256]{4,3,2,1,0:T(4,128)S(1)}, f32[1,4,16,4,256]{4,3,2,1,0:T(4,128)S(1)}, u32[]{:S(2)}, u32[]{:S(2)}) %collective-permute-start.5) | collective-permute-done | bytes 262176 | tf_op jit(solution)/shard_map/ppermute | solution.py:27
  95.9 1.0 fusion.32
  97.5 1.7 %collective-permute-start.7 = (f32[1,16,4,1024]{3,2,1,0:T(4,128)S(1)}, f32[1,16,4,1024]{3,2,1,0:T(4,128)S(1)}, u32[]{:S(2)}, u32[]{:S(2)}) collective-permute-start(f32[1,16,4,1024]{3,2,1,0:T(4,128)S(1)} %get-tuple-element.31), channel_id=1, source_target_pairs={{0,24},{8,0},{16,8},{24,16},{1,25},{9,1},{17,9},{25,17},{2,26},{10... | collective-permute-start | bytes 786440 | tf_op jit(solution)/shard_map/ppermute | solution.py:27
  99.8 11.4 %collective-permute-done.7 = f32[1,16,4,1024]{3,2,1,0:T(4,128)S(1)} collective-permute-done((f32[1,16,4,1024]{3,2,1,0:T(4,128)S(1)}, f32[1,16,4,1024]{3,2,1,0:T(4,128)S(1)}, u32[]{:S(2)}, u32[]{:S(2)}) %collective-permute-start.7) | collective-permute-done | bytes 262176 | tf_op jit(solution)/shard_map/ppermute | solution.py:27
  111.2 0.9 collective-permute-done.9
  112.1 7.3 %collective-permute-done.8 = f32[1,16,4,1024]{3,2,1,0:T(4,128)S(1)} collective-permute-done((f32[1,16,4,1024]{3,2,1,0:T(4,128)S(1)}, f32[1,16,4,1024]{3,2,1,0:T(4,128)S(1)}, u32[]{:S(2)}, u32[]{:S(2)}) %collective-permute-start.8) | collective-permute-done | bytes 262176 | tf_op jit(solution)/shard_map/ppermute | solution.py:27
  119.4 0.9 fusion.30
  (18 shorter events, 1.4 us)
Async XLA Ops:
  0.0 49.6 %copy-start = (bf16[1,96,128,128]{3,2,1,0:T(8,128)(2,1)S(1)}, bf16[1,96,128,128]{3,2,1,0:T(8,128)(2,1)}, u32[]{:S(2)}) copy-start(bf16[1,96,128,128]{3,2,1,0:T(8,128)(2,1)} %param.11) | copy-start | bytes 9437188
  1.4 10.0 %collective-permute-start = (bf16[1,16,4,1024]{3,2,1,0:T(4,128)(2,1)S(1)}, bf16[1,16,4,1024]{3,2,1,0:T(4,128)(2,1)S(1)}, u32[]{:S(2)}, u32[]{:S(2)}) collective-permute-start(bf16[1,16,4,1024]{3,2,1,0:T(4,128)(2,1)S(1)} %get-tuple-element.37), channel_id=1, source_target_pairs={{0,8},{8,16},{16,24},{24,0},{1,9},{9,17},{17,25},{25,1},{2,10},{10... | collective-permute-start | bytes 393224 | tf_op jit(solution)/shard_map/ppermute | solution.py:27
  4.5 7.8 %collective-permute-start.2 = (bf16[1,16,4,1024]{3,2,1,0:T(4,128)(2,1)S(1)}, bf16[1,16,4,1024]{3,2,1,0:T(4,128)(2,1)S(1)}, u32[]{:S(2)}, u32[]{:S(2)}) collective-permute-start(bf16[1,16,4,1024]{3,2,1,0:T(4,128)(2,1)S(1)} %get-tuple-element.38), channel_id=1, source_target_pairs={{0,24},{8,0},{16,8},{24,16},{1,25},{9,1},{17,9},{25,17},{2,26},{10... | collective-permute-start | bytes 393224 | tf_op jit(solution)/shard_map/ppermute | solution.py:27
  6.6 11.9 %collective-permute-start.1 = (bf16[1,16,4,1024]{3,2,1,0:T(4,128)(2,1)S(1)}, bf16[1,16,4,1024]{3,2,1,0:T(4,128)(2,1)S(1)}, u32[]{:S(2)}, u32[]{:S(2)}) collective-permute-start(bf16[1,16,4,1024]{3,2,1,0:T(4,128)(2,1)S(1)} %get-tuple-element.39), channel_id=1, source_target_pairs={{0,16},{8,24},{16,0},{24,8},{1,17},{9,25},{17,1},{25,9},{2,18},{10... | collective-permute-start | bytes 393224 | tf_op jit(solution)/shard_map/ppermute | solution.py:27
  18.6 5.3 %collective-permute-start.3 = (bf16[1,4,16,4,256]{4,3,2,1,0:T(4,128)(2,1)S(1)}, bf16[1,4,16,4,256]{4,3,2,1,0:T(4,128)(2,1)S(1)}, u32[]{:S(2)}, u32[]{:S(2)}) collective-permute-start(bf16[1,4,16,4,256]{4,3,2,1,0:T(4,128)(2,1)S(1)} %get-tuple-element.34), channel_id=1, source_target_pairs={{0,1},{1,2},{2,3},{3,4},{4,5},{5,6},{6,7},{7,0},{8,9},{9,10},{10,1... | collective-permute-start | bytes 393224 | tf_op jit(solution)/shard_map/ppermute | solution.py:16
  18.7 5.3 %collective-permute-start.4 = (bf16[1,4,16,4,256]{4,3,2,1,0:T(4,128)(2,1)S(1)}, bf16[1,4,16,4,256]{4,3,2,1,0:T(4,128)(2,1)S(1)}, u32[]{:S(2)}, u32[]{:S(2)}) collective-permute-start(bf16[1,4,16,4,256]{4,3,2,1,0:T(4,128)(2,1)S(1)} %get-tuple-element.35), channel_id=1, source_target_pairs={{1,0},{2,1},{3,2},{4,3},{5,4},{6,5},{7,6},{0,7},{9,8},{10,9},{11,1... | collective-permute-start | bytes 393224 | tf_op jit(solution)/shard_map/ppermute | solution.py:19
  43.4 6.2 %copy-start.1 = (f32[96,128]{1,0:T(8,128)S(1)}, f32[96,128]{1,0:T(8,128)}, u32[]{:S(2)}) copy-start(f32[96,128]{1,0:T(8,128)} %fusion.33) | copy-start | bytes 147460
  49.6 17.1 %copy-start.2 = (s32[1,96]{1,0:T(1,128)S(1)}, s32[1,96]{1,0:T(1,128)}, u32[]{:S(2)}) copy-start(s32[1,96]{1,0:T(1,128)} %param.12) | copy-start | bytes 1156
  86.8 9.1 %collective-permute-start.5 = (f32[1,4,16,4,256]{4,3,2,1,0:T(4,128)S(1)}, f32[1,4,16,4,256]{4,3,2,1,0:T(4,128)S(1)}, u32[]{:S(2)}, u32[]{:S(2)}) collective-permute-start(f32[1,4,16,4,256]{4,3,2,1,0:T(4,128)S(1)} %get-tuple-element.30), channel_id=1, source_target_pairs={{0,7},{1,0},{2,1},{3,2},{4,3},{5,4},{6,5},{7,6},{8,15},{9,8},{10,9... | collective-permute-start | bytes 786440 | tf_op jit(solution)/shard_map/ppermute | solution.py:27
  89.5 7.8 %collective-permute-start.6 = (f32[1,4,16,4,256]{4,3,2,1,0:T(4,128)S(1)}, f32[1,4,16,4,256]{4,3,2,1,0:T(4,128)S(1)}, u32[]{:S(2)}, u32[]{:S(2)}) collective-permute-start(f32[1,4,16,4,256]{4,3,2,1,0:T(4,128)S(1)} %get-tuple-element.29), channel_id=1, source_target_pairs={{0,1},{1,2},{2,3},{3,4},{4,5},{5,6},{6,7},{7,0},{8,9},{9,10},{10,1... | collective-permute-start | bytes 786440 | tf_op jit(solution)/shard_map/ppermute | solution.py:27
  97.5 13.7 %collective-permute-start.7 = (f32[1,16,4,1024]{3,2,1,0:T(4,128)S(1)}, f32[1,16,4,1024]{3,2,1,0:T(4,128)S(1)}, u32[]{:S(2)}, u32[]{:S(2)}) collective-permute-start(f32[1,16,4,1024]{3,2,1,0:T(4,128)S(1)} %get-tuple-element.31), channel_id=1, source_target_pairs={{0,24},{8,0},{16,8},{24,16},{1,25},{9,1},{17,9},{25,17},{2,26},{10... | collective-permute-start | bytes 786440 | tf_op jit(solution)/shard_map/ppermute | solution.py:27
  99.2 12.9 %collective-permute-start.9 = (f32[1,16,4,1024]{3,2,1,0:T(4,128)S(1)}, f32[1,16,4,1024]{3,2,1,0:T(4,128)S(1)}, u32[]{:S(2)}, u32[]{:S(2)}) collective-permute-start(f32[1,16,4,1024]{3,2,1,0:T(4,128)S(1)} %get-tuple-element.32), channel_id=1, source_target_pairs={{0,8},{8,16},{16,24},{24,0},{1,9},{9,17},{17,25},{25,1},{2,10},{10... | collective-permute-start | bytes 786440 | tf_op jit(solution)/shard_map/ppermute | solution.py:27
  99.5 19.9 %collective-permute-start.8 = (f32[1,16,4,1024]{3,2,1,0:T(4,128)S(1)}, f32[1,16,4,1024]{3,2,1,0:T(4,128)S(1)}, u32[]{:S(2)}, u32[]{:S(2)}) collective-permute-start(f32[1,16,4,1024]{3,2,1,0:T(4,128)S(1)} %get-tuple-element.33), channel_id=1, source_target_pairs={{0,16},{8,24},{16,0},{24,8},{1,17},{9,25},{17,1},{25,9},{2,18},{10... | collective-permute-start | bytes 786440 | tf_op jit(solution)/shard_map/ppermute | solution.py:27
where the time goes:
time: 121 us; the launch traced here: 120 us
  waiting for transfers between devices  34.1 us (28%)
  matrix products  33.4 us (28%)
  local copies, waits for them, and re-layouts  31 us (26%)
  starting transfers between devices  13.8 us (11%)
  other arithmetic  7.26 us (6%)
    ppermute x8, waiting for transfers between devices, passed_along(): return lax.ppermute(value, axis, pairs)  32.1 us
    dot_general x1, matrix products, observe(): jnp.einsum('bij,cbi->cbj', operator, misfit, preferred_element_type=jnp.f...  17.1 us
    dot_general x1, matrix products, observe(): jnp.einsum('cbj,bk->ckj', adjoint, selector, precision=lax.Precision.HIGH...  16.2 us
    ppermute x8, starting transfers between devices, passed_along(): return lax.ppermute(value, axis, pairs)  11.1 us
    gather x1, local copies, waits for them, and re-layouts, observe(): collected_entries = jnp.take(blocks, indices, axis=1)  7.11 us
    sub x1, local copies, waits for them, and re-layouts, observe(): misfit = ((images - observed) * scaling * live_mask).astype(jnp.bfloat16)  6.21 us
    mul x1, local copies, waits for them, and re-layouts, observe(): misfit = ((images - observed) * scaling * live_mask).astype(jnp.bfloat16)  6.1 us
    another operation x2, local copies, waits for them, and re-layouts, observe(): extended.reshape(-1, extended.shape[-1] // block_width, block_width)  4.96 us
  transfers between devices with their start and end apart: 10, of which 8 were waited for; matrix products, arithmetic and copies ran while one was open for 5% of the time, Pallas kernels for 0%

commit v1 on v0

v1 whole, which is shorter than its diff:
```python
import functools

import jax
import jax.numpy as jnp
from jax import lax
from jax.experimental import pallas as pl
from jax.experimental.pallas import tpu as pltpu
from jax.sharding import PartitionSpec as P

EDGE = 2
MESH = pl.DeviceIdType.MESH
VMEM = pl.BlockSpec(memory_space=pltpu.VMEM)
ANY = pl.BlockSpec(memory_space=pl.ANY)


def neighbours(space_size, shifts, tm_size):
    me_t, me_s = lax.axis_index("tm"), lax.axis_index("space")
    left = {"space": lax.rem(me_s + space_size - 1, space_size)}
    right = {"space": lax.rem(me_s + 1, space_size)}
    ahead = [{"tm": lax.rem(me_t + shift, tm_size)} for shift in shifts]
    behind = [{"tm": lax.rem(me_t + tm_size - shift, tm_size)} for shift in shifts]
    return left, right, ahead, behind


def greet(peers):
    barrier = pltpu.get_barrier_semaphore()
    for peer in peers:
        pl.semaphore_signal(barrier, inc=1, device_id=peer, device_id_type=MESH)
    pl.semaphore_wait(barrier, len(peers))


def gather_kernel(tm_size, space_size, shifts, x_ref, ext_ref, own_sem, send_sem, recv_sem):
    leads, cells = x_ref.shape[:2]
    left, right, ahead, _ = neighbours(space_size, shifts, tm_size)
    greet([left, right, *ahead])

    def send(src, dst, lead, slot, peer):
        copy = pltpu.make_async_remote_copy(
            src_ref=src,
            dst_ref=dst,
            send_sem=send_sem.at[lead, slot],
            recv_sem=recv_sem.at[lead, slot],
            device_id=peer,
            device_id_type=MESH,
        )
        copy.start()
        return copy

    parts = ((0, EDGE), (cells - EDGE, EDGE), (EDGE, cells - 2 * EDGE))
    sent = {}
    for slot, (begin, width) in enumerate(parts):
        for lead in range(1, leads):
            sent[lead, slot] = send(
                x_ref.at[lead, pl.ds(begin, width)],
                ext_ref.at[lead, pl.ds(begin + EDGE, width)],
                lead,
                slot,
                ahead[lead - 1],
            )
    own = pltpu.make_async_copy(x_ref.at[0], ext_ref.at[0, pl.ds(EDGE, cells)], own_sem)
    own.start()
    edges = [
        send(x_ref.at[0, pl.ds(0, EDGE)], ext_ref.at[0, pl.ds(cells + EDGE, EDGE)], 0, 3, left),
        send(x_ref.at[0, pl.ds(cells - EDGE, EDGE)], ext_ref.at[0, pl.ds(0, EDGE)], 0, 4, right),
    ]
    for slot in (0, 1):
        for lead in range(1, leads):
            sent[lead, slot].wait_recv()
            if slot == 0:
                src, dst, peer = pl.ds(EDGE, EDGE), pl.ds(cells + EDGE, EDGE), left
            else:
                src, dst, peer = pl.ds(cells, EDGE), pl.ds(0, EDGE), right
            edges.append(send(ext_ref.at[lead, src], ext_ref.at[lead, dst], lead, 3 + slot, peer))
    own.wait()
    for lead in range(1, leads):
        sent[lead, 2].wait_recv()
    for copy in edges:
        copy.wait()
    for copy in sent.values():
        copy.wait_send()


def observe_kernel(index_ref, count_ref, ext_ref, op_ref, value_ref, weight_ref, out_ref):
    chunk, width = op_ref.shape[:2]
    leads, _, rows, _ = ext_ref.shape
    step = pl.program_id(0)

    @pl.when(step == 0)
    def _():
        out_ref[...] = jnp.zeros_like(out_ref)

    repeat = 8 // value_ref.shape[0]
    for k in range(chunk):
        block = step * chunk + k
        cell = index_ref[block]
        fields = ext_ref[:, cell].reshape(leads * rows, width)
        operator = op_ref[k]
        images = lax.dot_general(
            fields, operator, (((1,), (1,)), ((), ())), preferred_element_type=jnp.float32
        )
        lanes = slice(k * width, (k + 1) * width)
        observed = value_ref[:, lanes].astype(jnp.float32)
        scaling = weight_ref[:, lanes].astype(jnp.float32)
        slot = block * width + lax.broadcasted_iota(jnp.int32, scaling.shape, 1)
        scaling = jnp.where(slot < count_ref[0], scaling, 0.0)
        observed = jnp.concatenate([observed] * repeat, axis=0)
        scaling = jnp.concatenate([scaling] * repeat, axis=0)
        departures = (images.reshape(-1, 8, width) - observed[None]) * scaling[None]
        misfit = departures.reshape(leads * rows, width).astype(jnp.bfloat16)
        adjoint = jnp.dot(misfit, operator, preferred_element_type=jnp.float32)
        out_ref[:, cell] += adjoint.reshape(leads, rows, width)


def return_kernel(
    tm_size, space_size, shifts, adj_ref, out_ref, below, above, part, staged, send_sem, recv_sem
):
    leads, wide, _, width = adj_ref.shape
    cells = wide - 2 * EDGE
    left, right, _, behind = neighbours(space_size, shifts, tm_size)
    greet([left, right, *behind])

    def send(src, dst, lead, slot, peer):
        copy = pltpu.make_async_remote_copy(
            src_ref=src,
            dst_ref=dst,
            send_sem=send_sem.at[lead, slot],
            recv_sem=recv_sem.at[lead, slot],
            device_id=peer,
            device_id_type=MESH,
        )
        copy.start()
        return copy

    low, high, copies = {}, {}, []
    order = [*range(1, leads), 0]
    for lead in order:
        high[lead] = send(adj_ref.at[lead, pl.ds(0, EDGE)], above.at[lead], lead, 0, left)
        low[lead] = send(adj_ref.at[lead, pl.ds(cells + EDGE, EDGE)], below.at[lead], lead, 1, right)
    for lead in order[:-1]:
        copies.append(
            send(
                adj_ref.at[lead, pl.ds(2 * EDGE, cells - 2 * EDGE)],
                part.at[lead - 1, pl.ds(EDGE, cells - 2 * EDGE)],
                lead,
                2,
                behind[lead - 1],
            )
        )
    for lead in order[:-1]:
        low[lead].wait_recv()
        staged[lead - 1, 0] = adj_ref[lead, EDGE : 2 * EDGE] + below[lead]
        copies.append(
            send(staged.at[lead - 1, 0], part.at[lead - 1, pl.ds(0, EDGE)], lead, 3, behind[lead - 1])
        )
        high[lead].wait_recv()
        staged[lead - 1, 1] = adj_ref[lead, cells : cells + EDGE] + above[lead]
        copies.append(
            send(
                staged.at[lead - 1, 1],
                part.at[lead - 1, pl.ds(cells - EDGE, EDGE)],
                lead,
                4,
                behind[lead - 1],
            )
        )
    low[0].wait_recv()
    high[0].wait_recv()
    for copy in copies:
        copy.wait_recv()
    for cell in range(cells):
        total = adj_ref[0, cell + EDGE]
        if cell < EDGE:
            total = total + below[0, cell]
        if cell >= cells - EDGE:
            total = total + above[0, cell - (cells - EDGE)]
        for lead in range(1, leads):
            total = total + part[lead - 1, cell]
        out_ref[:, cell * width : (cell + 1) * width] = total
    for copy in (*copies, *low.values(), *high.values()):
        copy.wait_send()


def body(mesh, hindcast_archive, op_blocks, block_index, obs_values, obs_weights, obs_counts):
    tm_size, space_size = mesh.shape["tm"], mesh.shape["space"]
    _, leads, members, layers, points = hindcast_archive.shape
    _, blocks, width, _ = op_blocks.shape
    rows, cells = members * layers, points // width
    wide = cells + 2 * EDGE
    shifts = [lead * tm_size // leads for lead in range(1, leads)]
    grouped = hindcast_archive.reshape(leads, rows, cells, width).transpose(0, 2, 1, 3)
    extended = pl.pallas_call(
        functools.partial(gather_kernel, tm_size, space_size, shifts),
        out_shape=jax.ShapeDtypeStruct((leads, wide, rows, width), jnp.bfloat16),
        in_specs=[ANY],
        out_specs=ANY,
        scratch_shapes=[
            pltpu.SemaphoreType.DMA,
            pltpu.SemaphoreType.DMA((leads, 5)),
            pltpu.SemaphoreType.DMA((leads, 5)),
        ],
        compiler_params=pltpu.CompilerParams(collective_id=0, has_side_effects=True),
    )(grouped)
    chunk = 16 if blocks % 16 == 0 else 1
    adjoint = pl.pallas_call(
        observe_kernel,
        out_shape=jax.ShapeDtypeStruct((leads, wide, rows, width), jnp.float32),
        grid_spec=pltpu.PrefetchScalarGridSpec(
            num_scalar_prefetch=2,
            grid=(blocks // chunk,),
            in_specs=[
                pl.BlockSpec((leads, wide, rows, width), lambda g, *_: (0, 0, 0, 0)),
                pl.BlockSpec((chunk, width, width), lambda g, *_: (g, 0, 0)),
                pl.BlockSpec((layers, chunk * width), lambda g, *_: (0, g)),
                pl.BlockSpec((layers, chunk * width), lambda g, *_: (0, g)),
            ],
            out_specs=pl.BlockSpec((leads, wide, rows, width), lambda g, *_: (0, 0, 0, 0)),
        ),
        compiler_params=pltpu.CompilerParams(vmem_limit_bytes=32 << 20),
    )(
        block_index[0],
        obs_counts[0],
        extended,
        op_blocks[0],
        obs_values[0],
        obs_weights[0],
    )
    gradient = pl.pallas_call(
        functools.partial(return_kernel, tm_size, space_size, shifts),
        out_shape=jax.ShapeDtypeStruct((rows, points), jnp.float32),
        in_specs=[VMEM],
        out_specs=VMEM,
        scratch_shapes=[
            pltpu.VMEM((leads, EDGE, rows, width), jnp.float32),
            pltpu.VMEM((leads, EDGE, rows, width), jnp.float32),
            pltpu.VMEM((leads - 1, cells, rows, width), jnp.float32),
            pltpu.VMEM((leads - 1, 2, EDGE, rows, width), jnp.float32),
            pltpu.SemaphoreType.DMA((leads, 5)),
            pltpu.SemaphoreType.DMA((leads, 5)),
        ],
        compiler_params=pltpu.CompilerParams(
            collective_id=1, has_side_effects=True, vmem_limit_bytes=32 << 20
        ),
    )(adjoint)
    return gradient.reshape(1, members, layers, points)


def solution(mesh):
    in_specs = (
        P("tm", None, None, None, "space"),
        P("tm", "space", None, None),
        P("tm", "space"),
        P("tm", None, "space"),
        P("tm", None, "space"),
        P("tm", "space"),
    )
    out_specs = P("tm", None, None, "space")
    return jax.shard_map(
        functools.partial(body, mesh),
        mesh=mesh,
        in_specs=in_specs,
        out_specs=out_specs,
        check_vma=False,
    )
```

time: 121 us -> 58 us (0.48)
  Pallas kernels: 0 us -> 50.7 us
  waiting for transfers between devices: 34.1 us -> 0 us
  matrix products: 33.4 us -> 0 us
  local copies, waits for them, and re-layouts: 31 us -> 6.17 us
  starting transfers between devices: 13.8 us -> 0 us
  other arithmetic: 7.26 us -> 0 us
    pallas_call x0 -> x3, Pallas kernels: none -> 50.7 us  [the longest x1 26.6 us: body(): pl.pallas_call(functools.partial(return_kernel, tm_size, space_size, shif...]
    ppermute x10 -> x0, waiting for transfers between devices: 34.1 us -> none  [the longest x8 32.1 us: passed_along(): return lax.ppermute(value, axis, pairs)]
    dot_general x2 -> x0, matrix products: 33.4 us -> none  [the longest x1 17.1 us: observe(): jnp.einsum('bij,cbi->cbj', operator, misfit, preferred_element_type=jnp.f...]
    ppermute x10 -> x0, starting transfers between devices: 13.8 us -> none  [the longest x8 11.1 us: passed_along(): return lax.ppermute(value, axis, pairs)]
    another operation x3 -> x0, local copies, waits for them, and re-layouts: 7.75 us -> none  [the longest x2 4.96 us: observe(): extended.reshape(-1, extended.shape[-1] // block_width, block_width)]
    gather x1 -> x0, local copies, waits for them, and re-layouts: 7.11 us -> none  [observe(): collected_entries = jnp.take(blocks, indices, axis=1)]
    sub x1 -> x0, local copies, waits for them, and re-layouts: 6.21 us -> none  [observe(): misfit = ((images - observed) * scaling * live_mask).astype(jnp.bfloat16)]
    mul x1 -> x0, local copies, waits for them, and re-layouts: 6.1 us -> none  [observe(): misfit = ((images - observed) * scaling * live_mask).astype(jnp.bfloat16)]
  transfers between devices with their start and end apart: 10 -> 0, of which waited for: 8 -> 0; matrix products, arithmetic and copies ran while one was open for 5% -> 0% of each run, Pallas kernels for 0% -> 0%
where the time goes in v1:
time: 58 us; the launch traced here: 57.8 us
  Pallas kernels  50.7 us (87%)
  local copies, waits for them, and re-layouts  6.17 us (11%)
  between operations  0.87 us (2%)
    pallas_call x1, Pallas kernels, body(): pl.pallas_call(functools.partial(return_kernel, tm_size, space_size, shif...  26.6 us
    pallas_call x1, Pallas kernels, body(): pl.pallas_call(functools.partial(gather_kernel, tm_size, space_size, shif...  17.7 us
    pallas_call x1, Pallas kernels, body(): pl.pallas_call(observe_kernel, out_shape=jax.ShapeDtypeStruct((leads, wid...  6.35 us
    reshape x2, local copies, waits for them, and re-layouts, body(): hindcast_archive.reshape(leads, rows, cells, width).transpose(0, 2, 1, 3)  4.26 us

profile of v1, /device:TPU:0, one launch (start us, length us, event | category | flops | bytes accessed | tf_op | source)
XLA Modules:
  0.0 57.8 jit_solution(7208872718719852979)
XLA Ops:
  0.0 0.0 copy-start.3
  0.0 0.0 copy-start.2
  0.0 0.0 copy-start.4
  0.0 0.0 copy-start.1
  0.8 2.3 %reshape.6 = bf16[4,64,8,128]{3,2,1,0:T(8,128)(2,1)} reshape(bf16[1,4,16,4,1024]{4,3,2,1,0:T(4,128)(2,1)} %param.6) | data formatting | bytes 1048576 | tf_op jit(solution)/shard_map/reshape | solution.py:190
  3.1 2.0 %copy.9 = bf16[4,64,8,128]{3,1,2,0:T(8,128)(2,1)} copy(bf16[4,64,8,128]{3,2,1,0:T(8,128)(2,1)} %reshape.6) | data formatting | bytes 1048576 | tf_op jit(solution)/shard_map/reshape | solution.py:190
  5.1 17.7 %shard_map.64.ext_ref = bf16[4,12,64,128]{3,2,1,0:T(8,128)(2,1)} custom-call(bf16[4,8,64,128]{3,2,1,0:T(8,128)(2,1)} %bitcast.13), custom_call_target="tpu_custom_call" | custom-call | tf_op jit(solution)/shard_map/pallas_call | solution.py:191
  22.8 0.0 copy-done.3
  22.8 0.0 copy-done.2
  22.8 0.0 copy-done.4
  22.9 0.0 copy-done.1
  22.9 0.0 copy-start
  22.9 1.1 %copy-done = bf16[4,12,64,128]{3,2,1,0:T(8,128)(2,1)S(1)} copy-done((bf16[4,12,64,128]{3,2,1,0:T(8,128)(2,1)S(1)}, bf16[4,12,64,128]{3,2,1,0:T(8,128)(2,1)}, u32[]{:S(2)}) %copy-start) | copy-done | bytes 786456
  24.0 6.4 %shard_map.65.adj_ref = f32[4,12,64,128]{3,2,1,0:T(8,128)S(1)} custom-call(s32[96]{0:T(128)S(1)} %bitcast.12, s32[1]{0:T(128)} %bitcast.8.count_ref, bf16[4,12,64,128]{3,2,1,0:T(8,128)(2,1)S(1)} %copy-done, bf16[96,128,128]{2,1,0:T(8,128)(2,1)S(1)} %bitcast.9, bf16[4,12288]{1,0:T(4,128)(2,1)S(1)} %bitcast.10, bf16[4,12288]{1,0:T(4,128)(2,1)S(1)} %bitcast.11), custom_call_target="tpu_custom_call" | custom-call | tf_op jit(solution)/shard_map/pallas_call | solution.py:204
  30.4 26.6 %shard_map.66 = f32[64,1024]{1,0:T(8,128)S(1)} custom-call(f32[4,12,64,128]{3,2,1,0:T(8,128)S(1)} %shard_map.65.adj_ref), custom_call_target="tpu_custom_call" | custom-call | tf_op jit(solution)/shard_map/pallas_call | solution.py:227
  57.0 0.8 %reshape.7 = f32[1,16,4,1024]{3,2,1,0:T(4,128)} reshape(f32[64,1024]{1,0:T(8,128)S(1)} %shard_map.66) | data formatting | bytes 524288 | tf_op jit(solution)/shard_map/reshape | solution.py:244
Async XLA Ops:
  0.0 22.8 %copy-start.3 = (bf16[1,4,12288]{2,1,0:T(4,128)(2,1)S(1)}, bf16[1,4,12288]{2,1,0:T(4,128)(2,1)}, u32[]{:S(2)}) copy-start(bf16[1,4,12288]{2,1,0:T(4,128)(2,1)} %param.10) | copy-start | bytes 294916
  0.0 22.8 %copy-start.2 = (bf16[1,4,12288]{2,1,0:T(4,128)(2,1)S(1)}, bf16[1,4,12288]{2,1,0:T(4,128)(2,1)}, u32[]{:S(2)}) copy-start(bf16[1,4,12288]{2,1,0:T(4,128)(2,1)} %param.9) | copy-start | bytes 294916
  0.0 22.8 %copy-start.4 = (s32[1,96]{1,0:T(1,128)S(1)}, s32[1,96]{1,0:T(1,128)}, u32[]{:S(2)}) copy-start(s32[1,96]{1,0:T(1,128)} %param.8) | copy-start | bytes 1156
  0.0 22.8 %copy-start.1 = (bf16[1,96,128,128]{3,2,1,0:T(8,128)(2,1)S(1)}, bf16[1,96,128,128]{3,2,1,0:T(8,128)(2,1)}, u32[]{:S(2)}) copy-start(bf16[1,96,128,128]{3,2,1,0:T(8,128)(2,1)} %param.7) | copy-start | bytes 9437188
  22.9 1.1 %copy-start = (bf16[4,12,64,128]{3,2,1,0:T(8,128)(2,1)S(1)}, bf16[4,12,64,128]{3,2,1,0:T(8,128)(2,1)}, u32[]{:S(2)}) copy-start(bf16[4,12,64,128]{3,2,1,0:T(8,128)(2,1)} %shard_map.64.ext_ref) | copy-start | bytes 2359300

commit v2 on v1

--- a/solution.py
+++ b/solution.py
@@ -8,6 +8,7 @@
 from jax.sharding import PartitionSpec as P
 
 EDGE = 2
+STEPS = 32767.0
 MESH = pl.DeviceIdType.MESH
 VMEM = pl.BlockSpec(memory_space=pltpu.VMEM)
 ANY = pl.BlockSpec(memory_space=pl.ANY)
@@ -29,8 +30,15 @@
     pl.semaphore_wait(barrier, len(peers))
 
 
-def gather_kernel(tm_size, space_size, shifts, x_ref, ext_ref, own_sem, send_sem, recv_sem):
-    leads, cells = x_ref.shape[:2]
+def gather_kernel(tm_size, space_size, shifts, raw_ref, ext_ref, x_ref, own_sem, send_sem, recv_sem):
+    leads, cells, rows, width = x_ref.shape
+
+    def regroup(lead):
+        for cell in range(cells):
+            lanes = slice(cell * width, (cell + 1) * width)
+            fields = raw_ref[lead, :, :, lanes].astype(jnp.float32)
+            x_ref[lead, cell] = fields.reshape(rows, width).astype(jnp.bfloat16)
+
     left, right, ahead, _ = neighbours(space_size, shifts, tm_size)
     greet([left, right, *ahead])
 
@@ -48,11 +56,12 @@
 
     parts = ((0, EDGE), (cells - EDGE, EDGE), (EDGE, cells - 2 * EDGE))
     sent = {}
-    for slot, (begin, width) in enumerate(parts):
-        for lead in range(1, leads):
+    for lead in (*range(1, leads), 0):
+        regroup(lead)
+        for slot, (begin, count) in enumerate(parts if lead else ()):
             sent[lead, slot] = send(
-                x_ref.at[lead, pl.ds(begin, width)],
-                ext_ref.at[lead, pl.ds(begin + EDGE, width)],
+                x_ref.at[lead, pl.ds(begin, count)],
+                ext_ref.at[lead, pl.ds(begin + EDGE, count)],
                 lead,
                 slot,
                 ahead[lead - 1],
@@ -111,8 +120,31 @@
         out_ref[:, cell] += adjoint.reshape(leads, rows, width)
 
 
+def encode(values, coded, scale):
+    most = jnp.max(jnp.abs(values), axis=0, keepdims=True)
+    most = jnp.maximum(most, 1e-30)
+    coded[...] = jnp.round(values * (STEPS / most)).astype(jnp.int32).astype(jnp.int16)
+    scale[...] = most * (1.0 / STEPS)
+
+
+def decode(coded, scale):
+    return coded.astype(jnp.int32).astype(jnp.float32) * scale
+
+
 def return_kernel(
-    tm_size, space_size, shifts, adj_ref, out_ref, below, above, part, staged, send_sem, recv_sem
+    tm_size,
+    space_size,
+    shifts,
+    adj_ref,
+    out_ref,
+    below,
+    above,
+    own_code,
+    own_scale,
+    part,
+    part_scale,
+    send_sem,
+    recv_sem,
 ):
     leads, wide, _, width = adj_ref.shape
     cells = wide - 2 * EDGE
@@ -136,45 +168,50 @@
     for lead in order:
         high[lead] = send(adj_ref.at[lead, pl.ds(0, EDGE)], above.at[lead], lead, 0, left)
         low[lead] = send(adj_ref.at[lead, pl.ds(cells + EDGE, EDGE)], below.at[lead], lead, 1, right)
+
+    def hand_back(lead, begin, count, slot):
+        span = pl.ds(begin, count)
+        for j, (own, other) in enumerate(((own_code, part), (own_scale, part_scale))):
+            copies.append(
+                send(
+                    own.at[lead - 1, span], other.at[lead - 1, span], lead, slot + j, behind[lead - 1]
+                )
+            )
+
     for lead in order[:-1]:
-        copies.append(
-            send(
-                adj_ref.at[lead, pl.ds(2 * EDGE, cells - 2 * EDGE)],
-                part.at[lead - 1, pl.ds(EDGE, cells - 2 * EDGE)],
-                lead,
-                2,
-                behind[lead - 1],
-            )
-        )
+        for cell in range(2 * EDGE, cells):
+            encode(adj_ref[lead, cell], own_code.at[lead - 1, cell], own_scale.at[lead - 1, cell])
+        hand_back(lead, 2 * EDGE, cells - 2 * EDGE, 2)
     for lead in order[:-1]:
         low[lead].wait_recv()
-        staged[lead - 1, 0] = adj_ref[lead, EDGE : 2 * EDGE] + below[lead]
-        copies.append(
-            send(staged.at[lead - 1, 0], part.at[lead - 1, pl.ds(0, EDGE)], lead, 3, behind[lead - 1])
-        )
         high[lead].wait_recv()
-        staged[lead - 1, 1] = adj_ref[lead, cells : cells + EDGE] + above[lead]
-        copies.append(
-            send(
-                staged.at[lead - 1, 1],
-                part.at[lead - 1, pl.ds(cells - EDGE, EDGE)],
-                lead,
-                4,
-                behind[lead - 1],
+        for e in range(EDGE):
+            encode(
+                adj_ref[lead, EDGE + e] + below[lead, e],
+                own_code.at[lead - 1, e],
+                own_scale.at[lead - 1, e],
             )
-        )
+            encode(
+                adj_ref[lead, cells + e] + above[lead, e],
+                own_code.at[lead - 1, EDGE + e],
+                own_scale.at[lead - 1, EDGE + e],
+            )
+        hand_back(lead, 0, 2 * EDGE, 4)
     low[0].wait_recv()
     high[0].wait_recv()
     for copy in copies:
         copy.wait_recv()
     for cell in range(cells):
         total = adj_ref[0, cell + EDGE]
+        place = cell + EDGE
         if cell < EDGE:
             total = total + below[0, cell]
+            place = cell
         if cell >= cells - EDGE:
             total = total + above[0, cell - (cells - EDGE)]
+            place = cell - (cells - EDGE) + EDGE
         for lead in range(1, leads):
-            total = total + part[lead - 1, cell]
+            total = total + decode(part[lead - 1, place], part_scale[lead - 1, place])
         out_ref[:, cell * width : (cell + 1) * width] = total
     for copy in (*copies, *low.values(), *high.values()):
         copy.wait_send()
@@ -187,19 +224,19 @@
     rows, cells = members * layers, points // width
     wide = cells + 2 * EDGE
     shifts = [lead * tm_size // leads for lead in range(1, leads)]
-    grouped = hindcast_archive.reshape(leads, rows, cells, width).transpose(0, 2, 1, 3)
     extended = pl.pallas_call(
         functools.partial(gather_kernel, tm_size, space_size, shifts),
         out_shape=jax.ShapeDtypeStruct((leads, wide, rows, width), jnp.bfloat16),
-        in_specs=[ANY],
+        in_specs=[VMEM],
         out_specs=ANY,
         scratch_shapes=[
+            pltpu.VMEM((leads, cells, rows, width), jnp.bfloat16),
             pltpu.SemaphoreType.DMA,
             pltpu.SemaphoreType.DMA((leads, 5)),
             pltpu.SemaphoreType.DMA((leads, 5)),
         ],
         compiler_params=pltpu.CompilerParams(collective_id=0, has_side_effects=True),
-    )(grouped)
+    )(hindcast_archive[0])
     chunk = 16 if blocks % 16 == 0 else 1
     adjoint = pl.pallas_call(
         observe_kernel,
@@ -232,10 +269,12 @@
         scratch_shapes=[
             pltpu.VMEM((leads, EDGE, rows, width), jnp.float32),
             pltpu.VMEM((leads, EDGE, rows, width), jnp.float32),
-            pltpu.VMEM((leads - 1, cells, rows, width), jnp.float32),
-            pltpu.VMEM((leads - 1, 2, EDGE, rows, width), jnp.float32),
-            pltpu.SemaphoreType.DMA((leads, 5)),
-            pltpu.SemaphoreType.DMA((leads, 5)),
+            pltpu.VMEM((leads - 1, cells, rows, width), jnp.int16),
+            pltpu.VMEM((leads - 1, cells, 1, width), jnp.float32),
+            pltpu.VMEM((leads - 1, cells, rows, width), jnp.int16),
+            pltpu.VMEM((leads - 1, cells, 1, width), jnp.float32),
+            pltpu.SemaphoreType.DMA((leads, 6)),
+            pltpu.SemaphoreType.DMA((leads, 6)),
         ],
         compiler_params=pltpu.CompilerParams(
             collective_id=1, has_side_effects=True, vmem_limit_bytes=32 << 20

time: 58 us -> 50 us (0.86)
  Pallas kernels: 50.7 us -> 42.7 us
    pallas_call x1, Pallas kernels: 26.6 us -> 17.9 us  [body(): pl.pallas_call(functools.partial(return_kernel, tm_size, space_size, shif...]
    unnamed x10, local copies, waits for them, and re-layouts: 1.14 us -> 5.45 us
    reshape x2 -> x0, local copies, waits for them, and re-layouts: 4.26 us -> none  [body(): hindcast_archive.reshape(leads, rows, cells, width).transpose(0, 2, 1, 3)]
    pallas_call x1, Pallas kernels: 17.7 us -> 18.4 us  [body(): pl.pallas_call(functools.partial(gather_kernel, tm_size, space_size, shif...]
where the time goes in v2:
time: 50 us; the launch traced here: 49.7 us
  Pallas kernels  42.7 us (85%)
  local copies, waits for them, and re-layouts  6.23 us (12%)
  between operations  0.69 us (1%)
    pallas_call x1, Pallas kernels, body(): pl.pallas_call(functools.partial(gather_kernel, tm_size, space_size, shif...  18.4 us
    pallas_call x1, Pallas kernels, body(): pl.pallas_call(functools.partial(return_kernel, tm_size, space_size, shif...  17.9 us
    pallas_call x1, Pallas kernels, body(): pl.pallas_call(observe_kernel, out_shape=jax.ShapeDtypeStruct((leads, wid...  6.41 us
    unnamed x10, local copies, waits for them, and re-layouts  5.45 us

profile of v2, /device:TPU:0, one launch (start us, length us, event | category | flops | bytes accessed | tf_op | source)
XLA Modules:
  0.0 49.7 jit_solution(16476312142163419691)
XLA Ops:
  0.7 18.4 %shard_map.64.ext_ref = bf16[4,12,64,128]{3,2,1,0:T(8,128)(2,1)} custom-call(bf16[4,16,4,1024]{3,2,1,0:T(4,128)(2,1)} %bitcast.11), custom_call_target="tpu_custom_call" | custom-call | tf_op jit(solution)/shard_map/pallas_call | solution.py:227
  19.1 0.0 copy-start
  19.1 1.1 %copy-done = bf16[4,12,64,128]{3,2,1,0:T(8,128)(2,1)S(1)} copy-done((bf16[4,12,64,128]{3,2,1,0:T(8,128)(2,1)S(1)}, bf16[4,12,64,128]{3,2,1,0:T(8,128)(2,1)}, u32[]{:S(2)}) %copy-start) | copy-done | bytes 786456
  20.2 0.0 copy-start.1
  20.2 1.9 %copy-done.1 = bf16[1,96,128,128]{3,2,1,0:T(8,128)(2,1)S(1)} copy-done((bf16[1,96,128,128]{3,2,1,0:T(8,128)(2,1)S(1)}, bf16[1,96,128,128]{3,2,1,0:T(8,128)(2,1)}, u32[]{:S(2)}) %copy-start.1) | copy-done | bytes 3145752
  22.1 0.0 copy-start.2
  22.1 0.9 %copy-done.2 = bf16[1,4,12288]{2,1,0:T(4,128)(2,1)S(1)} copy-done((bf16[1,4,12288]{2,1,0:T(4,128)(2,1)S(1)}, bf16[1,4,12288]{2,1,0:T(4,128)(2,1)}, u32[]{:S(2)}) %copy-start.2) | copy-done | bytes 98328
  23.0 0.0 copy-start.3
  23.0 0.9 %copy-done.3 = bf16[1,4,12288]{2,1,0:T(4,128)(2,1)S(1)} copy-done((bf16[1,4,12288]{2,1,0:T(4,128)(2,1)S(1)}, bf16[1,4,12288]{2,1,0:T(4,128)(2,1)}, u32[]{:S(2)}) %copy-start.3) | copy-done | bytes 98328
  23.9 0.0 copy-start.4
  23.9 0.7 %copy-done.4 = s32[1,96]{1,0:T(1,128)S(1)} copy-done((s32[1,96]{1,0:T(1,128)S(1)}, s32[1,96]{1,0:T(1,128)}, u32[]{:S(2)}) %copy-start.4) | copy-done | bytes 408
  24.6 6.4 %shard_map.65.adj_ref = f32[4,12,64,128]{3,2,1,0:T(8,128)S(1)} custom-call(s32[96]{0:T(128)S(1)} %bitcast.10, s32[1]{0:T(128)} %bitcast.6.count_ref, bf16[4,12,64,128]{3,2,1,0:T(8,128)(2,1)S(1)} %copy-done, bf16[96,128,128]{2,1,0:T(8,128)(2,1)S(1)} %bitcast.7, bf16[4,12288]{1,0:T(4,128)(2,1)S(1)} %bitcast.8, bf16[4,12288]{1,0:T(4,128)(2,1)S(1)} %bitcast.9), custom_call_target="tpu_custom_call" | custom-call | tf_op jit(solution)/shard_map/pallas_call | solution.py:241
  31.0 17.9 %shard_map.66 = f32[64,1024]{1,0:T(8,128)S(1)} custom-call(f32[4,12,64,128]{3,2,1,0:T(8,128)S(1)} %shard_map.65.adj_ref), custom_call_target="tpu_custom_call" | custom-call | tf_op jit(solution)/shard_map/pallas_call | solution.py:264
  48.9 0.8 %reshape.3 = f32[1,16,4,1024]{3,2,1,0:T(4,128)} reshape(f32[64,1024]{1,0:T(8,128)S(1)} %shard_map.66) | data formatting | bytes 524288 | tf_op jit(solution)/shard_map/reshape | solution.py:283
Async XLA Ops:
  19.1 1.1 %copy-start = (bf16[4,12,64,128]{3,2,1,0:T(8,128)(2,1)S(1)}, bf16[4,12,64,128]{3,2,1,0:T(8,128)(2,1)}, u32[]{:S(2)}) copy-start(bf16[4,12,64,128]{3,2,1,0:T(8,128)(2,1)} %shard_map.64.ext_ref) | copy-start | bytes 2359300
  20.2 1.9 %copy-start.1 = (bf16[1,96,128,128]{3,2,1,0:T(8,128)(2,1)S(1)}, bf16[1,96,128,128]{3,2,1,0:T(8,128)(2,1)}, u32[]{:S(2)}) copy-start(bf16[1,96,128,128]{3,2,1,0:T(8,128)(2,1)} %param.7) | copy-start | bytes 9437188
  22.1 0.9 %copy-start.2 = (bf16[1,4,12288]{2,1,0:T(4,128)(2,1)S(1)}, bf16[1,4,12288]{2,1,0:T(4,128)(2,1)}, u32[]{:S(2)}) copy-start(bf16[1,4,12288]{2,1,0:T(4,128)(2,1)} %param.9) | copy-start | bytes 294916
  23.0 0.9 %copy-start.3 = (bf16[1,4,12288]{2,1,0:T(4,128)(2,1)S(1)}, bf16[1,4,12288]{2,1,0:T(4,128)(2,1)}, u32[]{:S(2)}) copy-start(bf16[1,4,12288]{2,1,0:T(4,128)(2,1)} %param.10) | copy-start | bytes 294916
  23.9 0.7 %copy-start.4 = (s32[1,96]{1,0:T(1,128)S(1)}, s32[1,96]{1,0:T(1,128)}, u32[]{:S(2)}) copy-start(s32[1,96]{1,0:T(1,128)} %param.8) | copy-start | bytes 1156

commit v3 on v0

v3 whole, which is shorter than its diff:
```python
import functools

import jax
import jax.numpy as jnp
from jax import lax
from jax.experimental import pallas as pl
from jax.experimental.pallas import tpu as pltpu
from jax.sharding import PartitionSpec as P

EDGE = 2
PARTS = 2
CHUNK = 8
STEPS = 32767.0
MESH = pl.DeviceIdType.MESH
VMEM = pl.BlockSpec(memory_space=pltpu.VMEM)
HBM = pl.BlockSpec(memory_space=pltpu.HBM)


def neighbours(space_size, shifts, tm_size):
    me_t, me_s = lax.axis_index("tm"), lax.axis_index("space")
    left = {"space": lax.rem(me_s + space_size - 1, space_size)}
    right = {"space": lax.rem(me_s + 1, space_size)}
    ahead = [{"tm": lax.rem(me_t + shift, tm_size)} for shift in shifts]
    behind = [{"tm": lax.rem(me_t + tm_size - shift, tm_size)} for shift in shifts]
    return left, right, ahead, behind


def greet(peers):
    barrier = pltpu.get_barrier_semaphore()
    for peer in peers:
        pl.semaphore_signal(barrier, inc=1, device_id=peer, device_id_type=MESH)
    pl.semaphore_wait(barrier, len(peers))


def encode(values, coded, scale):
    most = jnp.max(jnp.abs(values), axis=0, keepdims=True)
    most = jnp.maximum(most, 1e-30)
    coded[...] = jnp.round(values * (STEPS / most)).astype(jnp.int32).astype(jnp.int16)
    scale[...] = most * (1.0 / STEPS)


def decode(coded, scale):
    return coded.astype(jnp.int32).astype(jnp.float32) * scale


def fused_kernel(
    tm_size,
    space_size,
    shifts,
    parts,
    index_ref,
    prev_ref,
    last_ref,
    count_ref,
    raw_hbm,
    op_hbm,
    value_hbm,
    weight_hbm,
    out_ref,
    raw_ref,
    op_ref,
    value_ref,
    weight_ref,
    x_ref,
    sums,
    adj,
    above,
    below,
    own_code,
    own_scale,
    part,
    part_scale,
    load_sem,
    go_send,
    go_recv,
    back_send,
    back_recv,
    *extended,
):
    _, leads, cells, rows, width = x_ref.shape
    blocks = op_ref.shape[0]
    members = raw_ref.shape[1] // parts
    wide = cells + 2 * EDGE
    left, right, ahead, behind = neighbours(space_size, shifts, tm_size)

    order = [*range(1, leads), 0]
    raw_loads = {
        lead: pltpu.make_async_copy(raw_hbm.at[lead], raw_ref.at[lead], load_sem.at[3 + lead])
        for lead in order
    }
    loads = [
        pltpu.make_async_copy(op_hbm, op_ref, load_sem.at[0]),
        pltpu.make_async_copy(value_hbm, value_ref, load_sem.at[1]),
        pltpu.make_async_copy(weight_hbm, weight_ref, load_sem.at[2]),
    ]
    for load in (*raw_loads.values(), *loads):
        load.start()
    sums[blocks] = jnp.zeros(sums.shape[1:], sums.dtype)
    greet([left, right, *ahead])

    def sender(send_sem, recv_sem):
        def send(src, dst, place, peer):
            copy = pltpu.make_async_remote_copy(
                src_ref=src,
                dst_ref=dst,
                send_sem=send_sem.at[place],
                recv_sem=recv_sem.at[place],
                device_id=peer,
                device_id_type=MESH,
            )
            copy.start()
            return copy

        return send

    go, back = sender(go_send, go_recv), sender(back_send, back_recv)
    pieces = ((0, EDGE), (cells - EDGE, EDGE), (EDGE, cells - 2 * EDGE))
    sent, edges = {}, {}
    for h in range(parts):
        for lead in order:
            if h == 0:
                raw_loads[lead].wait()
            for cell in range(cells):
                lanes = slice(cell * width, (cell + 1) * width)
                fields = raw_ref[lead, h * members : (h + 1) * members, :, lanes].astype(jnp.float32)
                fields = fields.reshape(rows, width).astype(jnp.bfloat16)
                x_ref[h, lead, cell] = fields
                if lead == 0:
                    extended[h][0, cell + EDGE] = fields
            for slot, (begin, span) in enumerate(pieces if lead else ()):
                sent[h, lead, slot] = go(
                    x_ref.at[h, lead, pl.ds(begin, span)],
                    extended[h].at[lead, pl.ds(begin + EDGE, span)],
                    (h, lead, slot),
                    ahead[lead - 1],
                )
        edges[h, 0, 0] = go(
            x_ref.at[h, 0, pl.ds(0, EDGE)],
            extended[h].at[0, pl.ds(cells + EDGE, EDGE)],
            (h, 0, 3),
            left,
        )
        edges[h, 0, 1] = go(
            x_ref.at[h, 0, pl.ds(cells - EDGE, EDGE)],
            extended[h].at[0, pl.ds(0, EDGE)],
            (h, 0, 4),
            right,
        )

    def forward_edges(h):
        for lead in range(1, leads):
            for slot in (0, 1):
                sent[h, lead, slot].wait_recv()
                if slot == 0:
                    src, dst, peer = pl.ds(EDGE, EDGE), pl.ds(cells + EDGE, EDGE), left
                else:
                    src, dst, peer = pl.ds(cells, EDGE), pl.ds(0, EDGE), right
                edges[h, lead, slot] = go(
                    extended[h].at[lead, src], extended[h].at[lead, dst], (h, lead, 3 + slot), peer
                )

    def await_fields(h):
        for lead in range(1, leads):
            sent[h, lead, 2].wait_recv()
        for lead in range(leads):
            for slot in (0, 1):
                edges[h, lead, slot].wait_recv()

    repeat = 8 // value_ref.shape[0]

    def observe(h, begin, end):
        def chunk(step, carry):
            for k in range(CHUNK):
                block = step * CHUNK + k
                operator = op_ref[block]
                fields = extended[h][:, index_ref[block]].reshape(leads * rows, width)
                images = lax.dot_general(
                    fields, operator, (((1,), (1,)), ((), ())), preferred_element_type=jnp.float32
                )
                lanes = pl.ds(pl.multiple_of(block * width, width), width)
                observed = value_ref[:, lanes].astype(jnp.float32)
                scaling = weight_ref[:, lanes].astype(jnp.float32)
                slot = block * width + lax.broadcasted_iota(jnp.int32, scaling.shape, 1)
                scaling = jnp.where(slot < count_ref[0], scaling, 0.0)
                observed = jnp.concatenate([observed] * repeat, axis=0)
                scaling = jnp.concatenate([scaling] * repeat, axis=0)
                departures = (images.reshape(-1, 8, width) - observed[None]) * scaling[None]
                misfit = departures.reshape(leads * rows, width).astype(jnp.bfloat16)
                adjoint = jnp.dot(misfit, operator, preferred_element_type=jnp.float32)
                sums[block] = adjoint + sums[prev_ref[block]]
            return carry

        lax.fori_loop(begin // CHUNK, end // CHUNK, chunk, 0)

    low, high, copies = {}, {}, []

    def hand_back(h, lead, begin, span, slot):
        span = pl.ds(begin, span)
        for j, (own, other) in enumerate(((own_code, part), (own_scale, part_scale))):
            copies.append(
                back(
                    own.at[h, lead - 1, span],
                    other.at[h, lead - 1, span],
                    (h, lead, slot + j),
                    behind[lead - 1],
                )
            )

    def put(h, lead, place, values):
        encode(values, own_code.at[h, lead - 1, place], own_scale.at[h, lead - 1, place])

    def return_middle(h):
        for cell in (*range(EDGE), *range(cells + EDGE, wide), *range(EDGE, cells + EDGE)):
            adj[h, :, cell] = sums[last_ref[cell]].reshape(leads, rows, width)
        for lead in order:
            high[h, lead] = back(adj.at[h, lead, pl.ds(0, EDGE)], above.at[h, lead], (h, lead, 0), left)
            low[h, lead] = back(
                adj.at[h, lead, pl.ds(cells + EDGE, EDGE)], below.at[h, lead], (h, lead, 1), right
            )
        for lead in order[:-1]:
            for cell in range(2 * EDGE, cells):
                put(h, lead, cell, adj[h, lead, cell])
            hand_back(h, lead, 2 * EDGE, cells - 2 * EDGE, 2)

    def return_edges(h):
        for lead in order[:-1]:
            low[h, lead].wait_recv()
            high[h, lead].wait_recv()
            for e in range(EDGE):
                put(h, lead, e, adj[h, lead, EDGE + e] + below[h, lead, e])
                put(h, lead, EDGE + e, adj[h, lead, cells + e] + above[h, lead, e])
            hand_back(h, lead, 0, 2 * EDGE, 4)

    middle = blocks // 2 // CHUNK * CHUNK
    forward_edges(0)
    for load in loads:
        load.wait()
    for h in range(parts):
        await_fields(h)
        observe(h, 0, middle)
        if h + 1 < parts:
            forward_edges(h + 1)
        if h:
            return_edges(h - 1)
        observe(h, middle, blocks)
        return_middle(h)
    return_edges(parts - 1)
    for h in range(parts):
        low[h, 0].wait_recv()
        high[h, 0].wait_recv()
    for copy in copies:
        copy.wait_recv()
    for h in range(parts):
        for cell in range(cells):
            total = adj[h, 0, cell + EDGE]
            place = cell + EDGE
            if cell < EDGE:
                total = total + below[h, 0, cell]
                place = cell
            if cell >= cells - EDGE:
                total = total + above[h, 0, cell - (cells - EDGE)]
                place = cell - (cells - EDGE) + EDGE
            for lead in range(1, leads):
                total = total + decode(part[h, lead - 1, place], part_scale[h, lead - 1, place])
            out_ref[h * rows : (h + 1) * rows, cell * width : (cell + 1) * width] = total
    for copy in (*copies, *low.values(), *high.values(), *sent.values(), *edges.values()):
        copy.wait_send()


def links(index, wide):
    blocks = index.shape[0]
    order = lax.broadcasted_iota(jnp.int32, (blocks, blocks), 1)
    own = lax.broadcasted_iota(jnp.int32, (blocks, blocks), 0)
    same = (index[None, :] == index[:, None]) & (order < own)
    prev = jnp.max(jnp.where(same, order, -1), axis=1)
    cell = lax.broadcasted_iota(jnp.int32, (wide, blocks), 0)
    last = jnp.max(jnp.where(index[None, :] == cell, order[:wide], -1), axis=1)
    return jnp.where(prev < 0, blocks, prev), jnp.where(last < 0, blocks, last)


def body(mesh, hindcast_archive, op_blocks, block_index, obs_values, obs_weights, obs_counts):
    tm_size, space_size = mesh.shape["tm"], mesh.shape["space"]
    _, leads, members, layers, points = hindcast_archive.shape
    _, blocks, width, _ = op_blocks.shape
    cells = points // width
    rows = members * layers // PARTS
    wide = cells + 2 * EDGE
    shifts = [lead * tm_size // leads for lead in range(1, leads)]
    prev, last = links(block_index[0], wide)
    smem = pl.BlockSpec(memory_space=pltpu.SMEM)
    gradient = pl.pallas_call(
        functools.partial(fused_kernel, tm_size, space_size, shifts, PARTS),
        out_shape=jax.ShapeDtypeStruct((members * layers, points), jnp.float32),
        in_specs=[smem] * 4 + [HBM] * 4,
        out_specs=VMEM,
        scratch_shapes=[
            pltpu.VMEM(hindcast_archive.shape[1:], jnp.bfloat16),
            pltpu.VMEM(op_blocks.shape[1:], jnp.bfloat16),
            pltpu.VMEM(obs_values.shape[1:], jnp.bfloat16),
            pltpu.VMEM(obs_weights.shape[1:], jnp.bfloat16),
            pltpu.VMEM((PARTS, leads, cells, rows, width), jnp.bfloat16),
            pltpu.VMEM((blocks + 1, leads * rows, width), jnp.float32),
            pltpu.VMEM((PARTS, leads, wide, rows, width), jnp.float32),
            pltpu.VMEM((PARTS, leads, EDGE, rows, width), jnp.float32),
            pltpu.VMEM((PARTS, leads, EDGE, rows, width), jnp.float32),
            pltpu.VMEM((PARTS, leads - 1, cells, rows, width), jnp.int16),
            pltpu.VMEM((PARTS, leads - 1, cells, 1, width), jnp.float32),
            pltpu.VMEM((PARTS, leads - 1, cells, rows, width), jnp.int16),
            pltpu.VMEM((PARTS, leads - 1, cells, 1, width), jnp.float32),
            pltpu.SemaphoreType.DMA((3 + leads,)),
            pltpu.SemaphoreType.DMA((PARTS, leads, 5)),
            pltpu.SemaphoreType.DMA((PARTS, leads, 5)),
            pltpu.SemaphoreType.DMA((PARTS, leads, 6)),
            pltpu.SemaphoreType.DMA((PARTS, leads, 6)),
        ]
        + [pltpu.VMEM((leads, wide, rows, width), jnp.bfloat16)] * PARTS,
        compiler_params=pltpu.CompilerParams(
            collective_id=0, has_side_effects=True, vmem_limit_bytes=48 << 20
        ),
    )(
        block_index[0],
        prev,
        last,
        obs_counts[0],
        hindcast_archive[0],
        op_blocks[0],
        obs_values[0],
        obs_weights[0],
    )
    return gradient.reshape(1, members, layers, points)


def solution(mesh):
    in_specs = (
        P("tm", None, None, None, "space"),
        P("tm", "space", None, None),
        P("tm", "space"),
        P("tm", None, "space"),
        P("tm", None, "space"),
        P("tm", "space"),
    )
    out_specs = P("tm", None, None, "space")
    return jax.shard_map(
        functools.partial(body, mesh),
        mesh=mesh,
        in_specs=in_specs,
        out_specs=out_specs,
        check_vma=False,
    )
```

time: 121 us -> 70.2 us (0.58)
  Pallas kernels: 0 us -> 61.4 us
  waiting for transfers between devices: 34.1 us -> 0 us
  matrix products: 33.4 us -> 0 us
  local copies, waits for them, and re-layouts: 31 us -> 6.14 us
  starting transfers between devices: 13.8 us -> 0 us
  other arithmetic: 7.26 us -> 1.7 us
    pallas_call x0 -> x1, Pallas kernels: none -> 61.4 us  [body(): pl.pallas_call(functools.partial(fused_kernel, tm_size, space_size, shift...]
    ppermute x10 -> x0, waiting for transfers between devices: 34.1 us -> none  [the longest x8 32.1 us: passed_along(): return lax.ppermute(value, axis, pairs)]
    dot_general x2 -> x0, matrix products: 33.4 us -> none  [the longest x1 17.1 us: observe(): jnp.einsum('bij,cbi->cbj', operator, misfit, preferred_element_type=jnp.f...]
    ppermute x10 -> x0, starting transfers between devices: 13.8 us -> none  [the longest x8 11.1 us: passed_along(): return lax.ppermute(value, axis, pairs)]
    another operation x3 -> x0, local copies, waits for them, and re-layouts: 7.75 us -> none  [the longest x2 4.96 us: observe(): extended.reshape(-1, extended.shape[-1] // block_width, block_width)]
    gather x1 -> x0, local copies, waits for them, and re-layouts: 7.11 us -> none  [observe(): collected_entries = jnp.take(blocks, indices, axis=1)]
    sub x1 -> x0, local copies, waits for them, and re-layouts: 6.21 us -> none  [observe(): misfit = ((images - observed) * scaling * live_mask).astype(jnp.bfloat16)]
    mul x1 -> x0, local copies, waits for them, and re-layouts: 6.1 us -> none  [observe(): misfit = ((images - observed) * scaling * live_mask).astype(jnp.bfloat16)]
  transfers between devices with their start and end apart: 10 -> 0, of which waited for: 8 -> 0; matrix products, arithmetic and copies ran while one was open for 5% -> 0% of each run, Pallas kernels for 0% -> 0%
where the time goes in v3:
time: 70.2 us; the launch traced here: 69.9 us
  Pallas kernels  61.4 us (87%)
  local copies, waits for them, and re-layouts  6.14 us (9%)
  other arithmetic  1.7 us (2%)
    pallas_call x1, Pallas kernels, body(): pl.pallas_call(functools.partial(fused_kernel, tm_size, space_size, shift...  61.4 us
    unnamed x10, local copies, waits for them, and re-layouts  5.36 us

profile of v3, /device:TPU:0, one launch (start us, length us, event | category | flops | bytes accessed | tf_op | source)
XLA Modules:
  0.0 69.9 jit_solution(15584469298346217730)
XLA Ops:
  0.7 0.8 %fusion.1 = s32[12]{0:T(128)S(1)} fusion(s32[96]{0:T(128)} %bitcast.11), kind=kLoop, calls=%fused_computation.4 | loop fusion | flops 3444 | bytes 432 | tf_op jit(solution)/shard_map/reduce_max | solution.py:277
  1.4 0.9 %select_reduce_fusion = s32[96]{0:T(128)S(1)} fusion(s32[96]{0:T(128)} %bitcast.12), kind=kLoop, calls=%fused_computation | loop fusion | flops 45984 | bytes 768 | tf_op jit(solution)/shard_map/reduce_max | solution.py:275
  2.4 0.0 copy-start
  2.4 1.9 %copy-done = bf16[1,96,128,128]{3,2,1,0:T(8,128)(2,1)S(1)} copy-done((bf16[1,96,128,128]{3,2,1,0:T(8,128)(2,1)S(1)}, bf16[1,96,128,128]{3,2,1,0:T(8,128)(2,1)}, u32[]{:S(2)}) %copy-start) | copy-done | bytes 3145752
  4.3 0.0 copy-start.1
  4.3 1.0 %copy-done.1 = bf16[1,4,16,4,1024]{4,3,2,1,0:T(4,128)(2,1)S(1)} copy-done((bf16[1,4,16,4,1024]{4,3,2,1,0:T(4,128)(2,1)S(1)}, bf16[1,4,16,4,1024]{4,3,2,1,0:T(4,128)(2,1)}, u32[]{:S(2)}) %copy-start.1) | copy-done | bytes 524312
  5.3 0.0 copy-start.2
  5.3 0.9 %copy-done.2 = bf16[1,4,12288]{2,1,0:T(4,128)(2,1)S(1)} copy-done((bf16[1,4,12288]{2,1,0:T(4,128)(2,1)S(1)}, bf16[1,4,12288]{2,1,0:T(4,128)(2,1)}, u32[]{:S(2)}) %copy-start.2) | copy-done | bytes 98328
  6.2 0.0 copy-start.3
  6.2 0.9 %copy-done.3 = bf16[1,4,12288]{2,1,0:T(4,128)(2,1)S(1)} copy-done((bf16[1,4,12288]{2,1,0:T(4,128)(2,1)S(1)}, bf16[1,4,12288]{2,1,0:T(4,128)(2,1)}, u32[]{:S(2)}) %copy-start.3) | copy-done | bytes 98328
  7.1 0.0 copy-start.4
  7.1 0.7 copy-done.4
  7.7 61.4 %shard_map.64 = f32[64,1024]{1,0:T(8,128)S(1)} custom-call(s32[96]{0:T(128)S(1)} %bitcast.13, s32[96]{0:T(128)S(1)} %compare_select_fusion.1.prev_ref, s32[12]{0:T(128)S(1)} %compare_select_fusion.last_ref, s32[1]{0:T(128)} %bitcast.6.count_ref, bf16[4,16,4,1024]{3,2,1,0:T(4,128)(2,1)S(1)} %bitcast.8, bf16[96,128,128]{2,1,0:T(8,128)(2,1)S(1)} %bitcast.7, ...), custom_call_target="tpu_custom_call" | custom-call | tf_op jit(solution)/shard_map/pallas_call | solution.py:291
  69.1 0.8 %reshape.4 = f32[1,16,4,1024]{3,2,1,0:T(4,128)} reshape(f32[64,1024]{1,0:T(8,128)S(1)} %shard_map.64) | data formatting | bytes 524288 | tf_op jit(solution)/shard_map/reshape | solution.py:330
  (2 shorter events, 0.0 us)
Async XLA Ops:
  2.4 1.9 %copy-start = (bf16[1,96,128,128]{3,2,1,0:T(8,128)(2,1)S(1)}, bf16[1,96,128,128]{3,2,1,0:T(8,128)(2,1)}, u32[]{:S(2)}) copy-start(bf16[1,96,128,128]{3,2,1,0:T(8,128)(2,1)} %param.7) | copy-start | bytes 9437188
  4.3 1.0 %copy-start.1 = (bf16[1,4,16,4,1024]{4,3,2,1,0:T(4,128)(2,1)S(1)}, bf16[1,4,16,4,1024]{4,3,2,1,0:T(4,128)(2,1)}, u32[]{:S(2)}) copy-start(bf16[1,4,16,4,1024]{4,3,2,1,0:T(4,128)(2,1)} %param.6) | copy-start | bytes 1572868
  5.3 0.9 %copy-start.2 = (bf16[1,4,12288]{2,1,0:T(4,128)(2,1)S(1)}, bf16[1,4,12288]{2,1,0:T(4,128)(2,1)}, u32[]{:S(2)}) copy-start(bf16[1,4,12288]{2,1,0:T(4,128)(2,1)} %param.9) | copy-start | bytes 294916
  6.2 0.9 %copy-start.3 = (bf16[1,4,12288]{2,1,0:T(4,128)(2,1)S(1)}, bf16[1,4,12288]{2,1,0:T(4,128)(2,1)}, u32[]{:S(2)}) copy-start(bf16[1,4,12288]{2,1,0:T(4,128)(2,1)} %param.10) | copy-start | bytes 294916
  7.1 0.7 copy-start.4

commit v4 on v2

--- a/solution.py
+++ b/solution.py
@@ -252,7 +252,7 @@
             ],
             out_specs=pl.BlockSpec((leads, wide, rows, width), lambda g, *_: (0, 0, 0, 0)),
         ),
-        compiler_params=pltpu.CompilerParams(vmem_limit_bytes=32 << 20),
+        compiler_params=pltpu.CompilerParams(vmem_limit_bytes=63 << 20),
     )(
         block_index[0],
         obs_counts[0],

time: 50 us -> 48.7 us (0.974)
  local copies, waits for them, and re-layouts: 6.23 us -> 2.18 us
  Pallas kernels: 42.7 us -> 45.5 us
    unnamed x10 -> x2, local copies, waits for them, and re-layouts: 5.45 us -> 1.41 us
    pallas_call x1, Pallas kernels: 6.41 us -> 9.25 us  [body(): pl.pallas_call(observe_kernel, out_shape=jax.ShapeDtypeStruct((leads, wid...]
where the time goes in v4:
time: 48.7 us; the launch traced here: 48.4 us
  Pallas kernels  45.5 us (93%)
  local copies, waits for them, and re-layouts  2.18 us (4%)
  between operations  0.67 us (1%)
    pallas_call x1, Pallas kernels, body(): pl.pallas_call(functools.partial(gather_kernel, tm_size, space_size, shif...  18.4 us
    pallas_call x1, Pallas kernels, body(): pl.pallas_call(functools.partial(return_kernel, tm_size, space_size, shif...  17.8 us
    pallas_call x1, Pallas kernels, body(): pl.pallas_call(observe_kernel, out_shape=jax.ShapeDtypeStruct((leads, wid...  9.25 us
    unnamed x2, local copies, waits for them, and re-layouts  1.41 us

profile of v4, /device:TPU:0, one launch (start us, length us, event | category | flops | bytes accessed | tf_op | source)
XLA Modules:
  0.0 48.4 jit_solution(12312888265998145835)
XLA Ops:
  0.7 18.4 %shard_map.64.ext_ref = bf16[4,12,64,128]{3,2,1,0:T(8,128)(2,1)} custom-call(bf16[4,16,4,1024]{3,2,1,0:T(4,128)(2,1)} %bitcast.8), custom_call_target="tpu_custom_call" | custom-call | tf_op jit(solution)/shard_map/pallas_call | solution.py:227
  19.1 9.2 %shard_map.65.adj_ref = f32[4,12,64,128]{3,2,1,0:T(8,128)} custom-call(s32[96]{0:T(128)} %bitcast.11, s32[1]{0:T(128)} %bitcast.6.count_ref, bf16[4,12,64,128]{3,2,1,0:T(8,128)(2,1)} %shard_map.64.ext_ref, bf16[96,128,128]{2,1,0:T(8,128)(2,1)} %bitcast.7, bf16[4,12288]{1,0:T(4,128)(2,1)} %bitcast.9, bf16[4,12288]{1,0:T(4,128)(2,1)} %bitcast.10), custom_call_target="tpu_custom_call" | custom-call | tf_op jit(solution)/shard_map/pallas_call | solution.py:241
  28.3 0.0 copy-start
  28.3 1.4 %copy-done = f32[4,12,64,128]{3,2,1,0:T(8,128)S(1)} copy-done((f32[4,12,64,128]{3,2,1,0:T(8,128)S(1)}, f32[4,12,64,128]{3,2,1,0:T(8,128)}, u32[]{:S(2)}) %copy-start) | copy-done | bytes 1572888
  29.7 17.8 %shard_map.66 = f32[64,1024]{1,0:T(8,128)S(1)} custom-call(f32[4,12,64,128]{3,2,1,0:T(8,128)S(1)} %copy-done), custom_call_target="tpu_custom_call" | custom-call | tf_op jit(solution)/shard_map/pallas_call | solution.py:264
  47.6 0.8 %reshape.3 = f32[1,16,4,1024]{3,2,1,0:T(4,128)} reshape(f32[64,1024]{1,0:T(8,128)S(1)} %shard_map.66) | data formatting | bytes 524288 | tf_op jit(solution)/shard_map/reshape | solution.py:283
Async XLA Ops:
  28.3 1.4 %copy-start = (f32[4,12,64,128]{3,2,1,0:T(8,128)S(1)}, f32[4,12,64,128]{3,2,1,0:T(8,128)}, u32[]{:S(2)}) copy-start(f32[4,12,64,128]{3,2,1,0:T(8,128)} %shard_map.65.adj_ref) | copy-start | bytes 4718596

commit v5 on v4

--- a/solution.py
+++ b/solution.py
@@ -237,7 +237,7 @@
         ],
         compiler_params=pltpu.CompilerParams(collective_id=0, has_side_effects=True),
     )(hindcast_archive[0])
-    chunk = 16 if blocks % 16 == 0 else 1
+    chunk = 32 if blocks % 32 == 0 else 1
     adjoint = pl.pallas_call(
         observe_kernel,
         out_shape=jax.ShapeDtypeStruct((leads, wide, rows, width), jnp.float32),

time: 48.7 us -> 47.3 us (0.971)
  Pallas kernels: 45.5 us -> 44.2 us
    pallas_call x1, Pallas kernels: 9.25 us -> 7.94 us  [body(): pl.pallas_call(observe_kernel, out_shape=jax.ShapeDtypeStruct((leads, wid...]
where the time goes in v5:
time: 47.3 us; the launch traced here: 47.1 us
  Pallas kernels  44.2 us (93%)
  local copies, waits for them, and re-layouts  2.18 us (5%)
  between operations  0.67 us (1%)
    pallas_call x1, Pallas kernels, body(): pl.pallas_call(functools.partial(gather_kernel, tm_size, space_size, shif...  18.4 us
    pallas_call x1, Pallas kernels, body(): pl.pallas_call(functools.partial(return_kernel, tm_size, space_size, shif...  17.8 us
    pallas_call x1, Pallas kernels, body(): pl.pallas_call(observe_kernel, out_shape=jax.ShapeDtypeStruct((leads, wid...  7.94 us
    unnamed x2, local copies, waits for them, and re-layouts  1.41 us

profile of v5, /device:TPU:0, one launch (start us, length us, event | category | flops | bytes accessed | tf_op | source)
XLA Modules:
  0.0 47.1 jit_solution(16612079681516613733)
XLA Ops:
  0.7 18.4 %shard_map.64.ext_ref = bf16[4,12,64,128]{3,2,1,0:T(8,128)(2,1)} custom-call(bf16[4,16,4,1024]{3,2,1,0:T(4,128)(2,1)} %bitcast.8), custom_call_target="tpu_custom_call" | custom-call | tf_op jit(solution)/shard_map/pallas_call | solution.py:227
  19.1 7.9 %shard_map.65.adj_ref = f32[4,12,64,128]{3,2,1,0:T(8,128)} custom-call(s32[96]{0:T(128)} %bitcast.11, s32[1]{0:T(128)} %bitcast.6.count_ref, bf16[4,12,64,128]{3,2,1,0:T(8,128)(2,1)} %shard_map.64.ext_ref, bf16[96,128,128]{2,1,0:T(8,128)(2,1)} %bitcast.7, bf16[4,12288]{1,0:T(4,128)(2,1)} %bitcast.9, bf16[4,12288]{1,0:T(4,128)(2,1)} %bitcast.10), custom_call_target="tpu_custom_call" | custom-call | tf_op jit(solution)/shard_map/pallas_call | solution.py:241
  27.0 0.0 copy-start
  27.0 1.4 %copy-done = f32[4,12,64,128]{3,2,1,0:T(8,128)S(1)} copy-done((f32[4,12,64,128]{3,2,1,0:T(8,128)S(1)}, f32[4,12,64,128]{3,2,1,0:T(8,128)}, u32[]{:S(2)}) %copy-start) | copy-done | bytes 1572888
  28.4 17.8 %shard_map.66 = f32[64,1024]{1,0:T(8,128)S(1)} custom-call(f32[4,12,64,128]{3,2,1,0:T(8,128)S(1)} %copy-done), custom_call_target="tpu_custom_call" | custom-call | tf_op jit(solution)/shard_map/pallas_call | solution.py:264
  46.3 0.8 %reshape.3 = f32[1,16,4,1024]{3,2,1,0:T(4,128)} reshape(f32[64,1024]{1,0:T(8,128)S(1)} %shard_map.66) | data formatting | bytes 524288 | tf_op jit(solution)/shard_map/reshape | solution.py:283
Async XLA Ops:
  27.0 1.4 %copy-start = (f32[4,12,64,128]{3,2,1,0:T(8,128)S(1)}, f32[4,12,64,128]{3,2,1,0:T(8,128)}, u32[]{:S(2)}) copy-start(f32[4,12,64,128]{3,2,1,0:T(8,128)} %shard_map.65.adj_ref) | copy-start | bytes 4718596
